TPU v7x, 32 devices: a whole 2x2x4 slice. The times are simulated.
32 devices in a mesh: section: 4 (over y, core), row: 4 (over z), col: 2 (over x).
Axes of the slice: x: 2, y: 2, z: 4, core: 2. Of those that a mesh axis runs over, the one named last changes fastest.
Arguments:
- inputs: bfloat16 [4, 768, 5120], P('section', 'row', 'col'), may hold values from -12 to 12
- down_weight: bfloat16 [4, 512, 5120], P('section', 'row', 'col'), may hold values from -5 to 5
- up_weight: bfloat16 [4, 512, 8192], P('section', 'row', 'col'), may hold values from -0.25 to 0.25
- value_grad: bfloat16 [4, 768, 8192], P('section', 'row', 'col'), may hold values from -1.1953125 to 1.1953125
Outputs:
- passed_grad: bfloat16 [4, 768, 5120], P('section', 'row', 'col')
- down_grad: bfloat16 [4, 512, 5120], P('section', 'row', 'col')
- up_grad: bfloat16 [4, 512, 8192], P('section', 'row', 'col')
All inputs are finite; a program needn't handle non-finite values.
Results may differ from a plain program's by a relative error of at most 0.03.
Values may be sent and summed in bfloat16 or wider, within the bound.
No kernel may reach another device: no remote copies, remote signals or barrier semaphores. Data moves between devices by JAX's collectives and lax.ppermute only.
A program may use at most 64 MiB of HBM per device.

v0:
```python
import jax
import jax.numpy as jnp
from jax import lax
from jax.sharding import PartitionSpec as P


def shifted(value, axis, steps):
    count = lax.axis_size(axis)
    leading, last = (max(0, -steps), min(count, count - steps))
    return lax.ppermute(value, axis, [(source, source + steps) for source in range(leading, last)])


def body(inputs, down_weight, up_weight, value_grad):
    tokens = inputs[0]
    cotangent = value_grad[0]
    down_full, up_full = (
        lax.all_gather(down_weight[0], "row", axis=0, tiled=True),
        lax.all_gather(up_weight[0], "row", axis=0, tiled=True),
    )
    latent_part = jnp.einsum("td,ld->tl", tokens, down_full, preferred_element_type=jnp.float32)
    grad_part = jnp.einsum("tf,lf->tl", cotangent, up_full, preferred_element_type=jnp.float32)
    latent, normed_grad = (
        lax.psum(latent_part.astype(jnp.bfloat16), "col").astype(jnp.float32),
        lax.psum(grad_part.astype(jnp.bfloat16), "col").astype(jnp.float32),
    )
    inv_rms = lax.rsqrt(jnp.mean(latent * latent, axis=-1, keepdims=True) + 1e-06)
    normed = latent * inv_rms
    normed_bf = normed.astype(jnp.bfloat16)
    inner = jnp.mean(normed_grad * normed, axis=-1, keepdims=True)
    latent_bf = (inv_rms * (normed_grad - normed * inner)).astype(jnp.bfloat16)
    picked = normed_bf
    up_grad = lax.psum_scatter(
        jnp.einsum("tl,tf->lf", picked, cotangent, preferred_element_type=jnp.float32).astype(
            jnp.bfloat16
        ),
        "row",
        scatter_dimension=0,
        tiled=True,
    )
    picked = latent_bf
    down_grad = lax.psum_scatter(
        jnp.einsum("tl,td->ld", picked, tokens, preferred_element_type=jnp.float32).astype(
            jnp.bfloat16
        ),
        "row",
        scatter_dimension=0,
        tiled=True,
    )
    input_grad = jnp.einsum(
        "tl,ld->td", latent_bf, down_full, preferred_element_type=jnp.float32
    ).astype(jnp.bfloat16)
    passed = shifted(input_grad, "section", -1)
    return (passed[None], down_grad[None], up_grad[None])


def solution(mesh):
    return jax.shard_map(
        body,
        mesh=mesh,
        in_specs=(
            P("section", "row", "col"),
            P("section", "row", "col"),
            P("section", "row", "col"),
            P("section", "row", "col"),
        ),
        out_specs=(
            P("section", "row", "col"),
            P("section", "row", "col"),
            P("section", "row", "col"),
        ),
        check_vma=False,
    )
```

profile of v0, /device:TPU:4, one launch (start us, length us, event | category | flops | bytes accessed | tf_op | source)
XLA Modules:
  0.0 320.8 jit_solution(17846282509824530930)
XLA Ops:
  7.2 0.0 copy-start
  7.2 0.0 all-gather.5.cloned.1.call-start
  7.2 0.7 all-gather.5.cloned.1.call-update
  7.9 0.0 all-gather.7.cloned.1.call-start
  8.0 0.7 all-gather.7.cloned.1.call-update
  8.7 0.0 all-reduce.3.cloned.1.call-start
  8.7 56.9 %all-gather.5.cloned.1.call-done = bf16[1,512,2560]{2,1,0:T(8,128)(2,1)} async-done(((bf16[1,128,2560]{2,1,0:T(8,128)(2,1)}), bf16[1,512,2560]{2,1,0:T(8,128)(2,1)}) %all-gather.5.cloned.1.call-update) | async-done | bytes 2621456 | tf_op jit(solution)/shard_map/all_gather | solution.py:17
  65.6 3.7 %fusion.7 = bf16[192,512]{1,0:T(8,128)(2,1)} fusion(bf16[1,512,2560]{2,1,0:T(8,128)(2,1)} %all-gather.5.cloned.1.call-done, bf16[1,192,2560]{2,1,0:T(8,128)(2,1)} %param.4), kind=kOutput, calls=%fused_computation.10 | convolution fusion | flops 503414784 | bytes 3801088 | tf_op jit(solution)/shard_map/td,ld->tl/dot_general | solution.py:20
  69.4 0.0 copy-start.2
  69.4 77.4 %all-gather.7.cloned.1.call-done = bf16[1,512,4096]{2,1,0:T(8,128)(2,1)} async-done(((bf16[1,128,4096]{2,1,0:T(8,128)(2,1)}), bf16[1,512,4096]{2,1,0:T(8,128)(2,1)}) %all-gather.7.cloned.1.call-update) | async-done | bytes 4194320 | tf_op jit(solution)/shard_map/all_gather | solution.py:18
  146.8 0.0 copy-done
  146.8 4.4 %fusion.10 = bf16[192,512]{1,0:T(8,128)(2,1)} fusion(bf16[1,512,4096]{2,1,0:T(8,128)(2,1)} %all-gather.7.cloned.1.call-done, bf16[1,192,4096]{2,1,0:T(8,128)(2,1)S(1)} %copy-done), kind=kOutput, calls=%fused_computation.11 | convolution fusion | flops 805404672 | bytes 5963776 | tf_op jit(solution)/shard_map/tf,lf->tl/dot_general | solution.py:21
  151.2 0.0 all-reduce.3.cloned.1.call-update
  151.2 0.0 reduce-scatter.3.cloned.1.call-start
  151.3 24.5 %all-reduce.3.cloned.1.call-done = (bf16[192,512]{1,0:T(8,128)(2,1)}, bf16[192,512]{1,0:T(8,128)(2,1)}) async-done(((bf16[192,512]{1,0:T(8,128)(2,1)}, bf16[192,512]{1,0:T(8,128)(2,1)}), (bf16[192,512]{1,0:T(8,128)(2,1)}, bf16[192,512]{1,0:T(8,128)(2,1)})) %all-reduce.3.cloned.1.call-update) | async-done | bytes 393232 | tf_op jit(solution)/shard_map/psum | solution.py:23
  175.8 1.0 fusion.19
  176.8 1.2 fusion.20
  178.1 0.0 copy-done.2
  178.1 0.0 copy-start.1
  178.1 3.6 %convolution_convert_fusion.1 = bf16[512,2560]{1,0:T(8,128)(2,1)} fusion(bf16[1,192,2560]{2,1,0:T(8,128)(2,1)S(1)} %copy-done.2, bf16[192,512]{1,0:T(8,128)(2,1)} %get-tuple-element.3, bf16[192,512]{1,0:T(8,128)(2,1)} %get-tuple-element.4, f32[192]{0:T(256)S(1)} %broadcast_multiply_fusion, f32[192]{0:T(256)S(1)} %add_rsqrt_fusion), kind=kOutput, calls=%fused_computation.1 | convolution fusion | flops 505315328 | bytes 3999232 | tf_op jit(solution)/shard_map/tl,td->ld/dot_general | solution.py:42
  181.7 0.0 reduce-scatter.3.cloned.1.call-update
  181.7 0.0 reduce-scatter.5.cloned.1.call-start
  181.8 0.0 copy-done.1
  181.8 3.3 %convolution_convert_fusion = bf16[512,4096]{1,0:T(8,128)(2,1)} fusion(bf16[1,192,4096]{2,1,0:T(8,128)(2,1)S(1)} %copy-done, bf16[192,512]{1,0:T(8,128)(2,1)S(1)} %copy-done.1, f32[192]{0:T(256)S(1)} %add_rsqrt_fusion), kind=kOutput, calls=%fused_computation | convolution fusion | flops 807698432 | bytes 5964544 | tf_op jit(solution)/shard_map/tl,tf->lf/dot_general | solution.py:33
  185.1 0.0 copy-start.3
  185.1 0.0 reduce-scatter.5.cloned.1.call-update
  185.1 0.9 copy-done.3
  186.0 2.5 convolution_convert_fusion.2
  188.5 1.9 collective-permute-start
  190.4 11.6 %collective-permute-done = bf16[192,2560]{1,0:T(8,128)(2,1)S(1)} collective-permute-done((bf16[192,2560]{1,0:T(8,128)(2,1)S(1)}, bf16[192,2560]{1,0:T(8,128)(2,1)S(1)}, u32[]{:S(2)}, u32[]{:S(2)}) %collective-permute-start) | collective-permute-done | bytes 983072 | tf_op jit(solution)/shard_map/ppermute | solution.py:10
  202.0 32.0 %reduce-scatter.3.cloned.1.call-done = bf16[128,2560]{1,0:T(8,128)(2,1)} async-done(((bf16[512,2560]{1,0:T(8,128)(2,1)}), bf16[128,2560]{1,0:T(8,128)(2,1)}) %reduce-scatter.3.cloned.1.call-update) | async-done | bytes 655376 | tf_op jit(solution)/shard_map/reduce_scatter | solution.py:41
  234.0 79.3 %reduce-scatter.5.cloned.1.call-done = bf16[128,4096]{1,0:T(8,128)(2,1)} async-done(((bf16[512,4096]{1,0:T(8,128)(2,1)}), bf16[128,4096]{1,0:T(8,128)(2,1)}) %reduce-scatter.5.cloned.1.call-update) | async-done | bytes 1048592 | tf_op jit(solution)/shard_map/reduce_scatter | solution.py:32
  313.3 0.9 copy.10
  (2 shorter events, 0.0 us)
Async XLA Ops:
  7.2 139.6 %copy-start = (bf16[1,192,4096]{2,1,0:T(8,128)(2,1)S(1)}, bf16[1,192,4096]{2,1,0:T(8,128)(2,1)}, u32[]{:S(2)}) copy-start(bf16[1,192,4096]{2,1,0:T(8,128)(2,1)} %param.7) | copy-start | bytes 4718596
  7.2 58.5 %all-gather.5.cloned.1.call-start = ((), (), s32[]{:S(2)}) async-start(), calls=%async_computation.4 | async-start | bytes 3276800 | tf_op jit(solution)/shard_map/all_gather | solution.py:17
  7.9 138.9 %all-gather.7.cloned.1.call-start = ((), (), s32[]{:S(2)}) async-start(), calls=%async_computation.5 | async-start | bytes 5242880 | tf_op jit(solution)/shard_map/all_gather | solution.py:18
  8.7 167.1 %all-reduce.3.cloned.1.call-start = ((), (), s32[]{:S(2)}) async-start(), calls=%async_computation.6 | async-start | bytes 786432 | tf_op jit(solution)/shard_map/psum | solution.py:23
  69.4 108.7 %copy-start.2 = (bf16[1,192,2560]{2,1,0:T(8,128)(2,1)S(1)}, bf16[1,192,2560]{2,1,0:T(8,128)(2,1)}, u32[]{:S(2)}) copy-start(bf16[1,192,2560]{2,1,0:T(8,128)(2,1)} %param.4) | copy-start | bytes 2949124
  151.2 82.8 %reduce-scatter.3.cloned.1.call-start = ((), (), s32[]{:S(2)}) async-start(), calls=%async_computation.2 | async-start | bytes 3276800 | tf_op jit(solution)/shard_map/reduce_scatter | solution.py:41
  178.1 3.7 %copy-start.1 = (bf16[192,512]{1,0:T(8,128)(2,1)S(1)}, bf16[192,512]{1,0:T(8,128)(2,1)}, u32[]{:S(2)}) copy-start(bf16[192,512]{1,0:T(8,128)(2,1)} %get-tuple-element.3) | copy-start | bytes 589828
  181.7 131.6 %reduce-scatter.5.cloned.1.call-start = ((), (), s32[]{:S(2)}) async-start(), calls=%async_computation.3 | async-start | bytes 5242880 | tf_op jit(solution)/shard_map/reduce_scatter | solution.py:32
  185.1 0.9 copy-start.3
  188.5 13.5 %collective-permute-start = (bf16[192,2560]{1,0:T(8,128)(2,1)S(1)}, bf16[192,2560]{1,0:T(8,128)(2,1)S(1)}, u32[]{:S(2)}, u32[]{:S(2)}) collective-permute-start(bf16[192,2560]{1,0:T(8,128)(2,1)S(1)} %convolution_convert_fusion.2), channel_id=1, source_target_pairs={{8,0},{16,8},{24,16},{9,1},{17,9},{25,17},{10,2},{18,10},{26,18},{... | collective-permute-start | bytes 2949128 | tf_op jit(solution)/shard_map/ppermute | solution.py:10
Sparse Core Ops, SparseCore 0:
  9.6 56.0 all-gather.4
  67.2 79.5 all-gather.6
  151.3 24.3 all-reduce.2
  181.9 52.1 reduce-scatter.2
  236.8 76.4 reduce-scatter.4
where the time goes:
time: 323 us; the launch traced here: 321 us
  waiting for transfers between devices  283 us (88%)
  matrix products  17.5 us (5%)
  between operations  13.8 us (4%)
    reduce_scatter x1, waiting for transfers between devices, body(): lax.psum_scatter(jnp.einsum('tl,tf->lf', picked, cotangent, preferred_ele...  79.3 us
    all_gather x1, waiting for transfers between devices, body(): lax.all_gather(up_weight[0], 'row', axis=0, tiled=True)  77.4 us
    all_gather x1, waiting for transfers between devices, body(): lax.all_gather(down_weight[0], 'row', axis=0, tiled=True)  56.9 us
    reduce_scatter x1, waiting for transfers between devices, body(): lax.psum_scatter(jnp.einsum('tl,td->ld', picked, tokens, preferred_elemen...  32 us
    psum x1, waiting for transfers between devices, body(): lax.psum(latent_part.astype(jnp.bfloat16), 'col').astype(jnp.float32)  24.5 us
    ppermute x1, waiting for transfers between devices, shifted(): lax.ppermute(value, axis, [(source, source + steps) for source in range(l...  11.6 us
  transfers between devices with their start and end apart: 6, of which 6 were waited for; matrix products, arithmetic and copies ran while one was open for 3% of the time, Pallas kernels for 0%

commit v1 on v0

v1 whole, which is shorter than its diff:
```python
import jax
import jax.numpy as jnp
from jax import lax
from jax.sharding import PartitionSpec as P

F32 = jnp.float32
BF16 = jnp.bfloat16
SLICES = 4


def shifted(value, axis, steps):
    count = lax.axis_size(axis)
    leading, last = (max(0, -steps), min(count, count - steps))
    return lax.ppermute(value, axis, [(source, source + steps) for source in range(leading, last)])


def general_body(inputs, down_weight, up_weight, value_grad):
    tokens = inputs[0]
    cotangent = value_grad[0]
    down_full = lax.all_gather(down_weight[0], "row", axis=0, tiled=True)
    up_full = lax.all_gather(up_weight[0], "row", axis=0, tiled=True)
    latent_part = jnp.einsum("td,ld->tl", tokens, down_full, preferred_element_type=F32)
    grad_part = jnp.einsum("tf,lf->tl", cotangent, up_full, preferred_element_type=F32)
    latent = lax.psum(latent_part.astype(BF16), "col").astype(F32)
    normed_grad = lax.psum(grad_part.astype(BF16), "col").astype(F32)
    inv_rms = lax.rsqrt(jnp.mean(latent * latent, axis=-1, keepdims=True) + 1e-06)
    normed = latent * inv_rms
    normed_bf = normed.astype(BF16)
    inner = jnp.mean(normed_grad * normed, axis=-1, keepdims=True)
    latent_bf = (inv_rms * (normed_grad - normed * inner)).astype(BF16)
    up_grad = lax.psum_scatter(
        jnp.einsum("tl,tf->lf", normed_bf, cotangent, preferred_element_type=F32).astype(BF16),
        "row",
        scatter_dimension=0,
        tiled=True,
    )
    down_grad = lax.psum_scatter(
        jnp.einsum("tl,td->ld", latent_bf, tokens, preferred_element_type=F32).astype(BF16),
        "row",
        scatter_dimension=0,
        tiled=True,
    )
    input_grad = jnp.einsum("tl,ld->td", latent_bf, down_full, preferred_element_type=F32)
    passed = shifted(input_grad.astype(BF16), "section", -1)
    return (passed[None], down_grad[None], up_grad[None])


def inward(value):
    return lax.ppermute(value, "row", [(0, 1), (3, 2)])


def across(value):
    return lax.ppermute(value, "row", [(1, 2), (2, 1)])


def outward(value):
    return lax.ppermute(value, "row", [(1, 0), (2, 3)])


def other_col(value):
    return lax.ppermute(value, "col", [(0, 1), (1, 0)])


def rows_dot(left, right):
    return lax.dot_general(left, right, (((1,), (1,)), ((), ())), preferred_element_type=F32)


def tokens_dot(left, right):
    return lax.dot_general(left, right, (((0,), (0,)), ((), ())), preferred_element_type=F32)


def col_sum(part):
    sent = part.astype(BF16)
    return sent.astype(F32) + other_col(sent).astype(F32)


def folded_body(inputs, down_weight, up_weight, value_grad):
    tokens, down, up, cotangent = inputs[0], down_weight[0], up_weight[0], value_grad[0]
    rows, width = tokens.shape
    lat = down.shape[0]
    feat = cotangent.shape[1]
    sections = lax.axis_size("section")
    place = lax.axis_index("row")
    middle = (place == 1) | (place == 2)

    down_end = inward(down)
    tokens_end = inward(tokens)
    down_other = across(down)
    down_other_end = across(down_end)

    pieces = []
    step = feat // SLICES
    for k in range(SLICES):
        cut = slice(k * step, (k + 1) * step)
        own = cotangent[:, cut]
        moved = inward(jnp.concatenate([own, up[:, cut]], axis=0))
        other = across(own)
        other_end = across(moved[:rows])
        pieces.append((
            jnp.concatenate([own, moved[:rows], other, other_end], axis=0),
            jnp.concatenate([up[:, cut], moved[rows:]], axis=0),
        ))

    tokens_mine = jnp.concatenate([tokens, tokens_end], axis=0)
    down_all = jnp.concatenate([down, down_end, down_other, down_other_end], axis=0)
    latent = col_sum(rows_dot(tokens_mine, down_all))
    inv_rms = lax.rsqrt(jnp.mean(latent * latent, axis=-1, keepdims=True) + 1e-06)
    normed = latent * inv_rms
    normed_bf = normed.astype(BF16)
    normed_all = jnp.concatenate(
        [normed_bf[:, : 2 * lat], across(normed_bf[:, 2 * lat :])], axis=0
    )

    grad_part = None
    up_pieces = []
    for values, weights in pieces:
        term = rows_dot(values, weights)
        grad_part = term if grad_part is None else grad_part + term
        up_piece = tokens_dot(normed_all, values).astype(BF16)
        back = outward(up_piece[lat:])
        up_pieces.append(jnp.where(middle, up_piece[:lat], back))
    up_grad = jnp.concatenate(up_pieces, axis=1)

    grad_mine = col_sum(grad_part[: 2 * rows])
    grad_other = col_sum(grad_part[2 * rows :])
    normed_grad = jnp.concatenate([grad_mine, across(grad_other.astype(BF16)).astype(F32)], axis=1)
    inner = jnp.mean(normed_grad * normed, axis=-1, keepdims=True)
    latent_bf = (inv_rms * (normed_grad - normed * inner)).astype(BF16)

    sums = [
        tokens_dot(latent_bf[:, j * lat : (j + 1) * lat], tokens_mine) for j in range(4)
    ]
    from_end = across(sums[3].astype(BF16))
    from_own = across(sums[2].astype(BF16))
    down_end_grad = outward((sums[1] + from_end.astype(F32)).astype(BF16))
    down_own_grad = (sums[0] + from_own.astype(F32)).astype(BF16)
    down_grad = jnp.where(middle, down_own_grad, down_end_grad)

    input_grad = jnp.dot(latent_bf, down_all, preferred_element_type=F32).astype(BF16)
    passed_own = shifted(input_grad[:rows], "section", -1)
    passed_end = lax.ppermute(
        input_grad[rows:],
        ("section", "row"),
        [
            (4 * s + source, 4 * (s - 1) + target)
            for s in range(1, sections)
            for source, target in ((1, 0), (2, 3))
        ],
    )
    passed = jnp.where(middle, passed_own, passed_end)
    return (passed[None], down_grad[None], up_grad[None])


def solution(mesh):
    spec = P("section", "row", "col")
    folds = mesh.shape["row"] == 4 and mesh.shape["col"] == 2
    return jax.shard_map(
        folded_body if folds else general_body,
        mesh=mesh,
        in_specs=(spec,) * 4,
        out_specs=(spec,) * 3,
        check_vma=False,
    )
```

time: 323 us -> 213 us (0.66)
  waiting for transfers between devices: 283 us -> 140 us
  starting transfers between devices: 2.12 us -> 51.5 us
  between operations: 13.8 us -> 1.72 us
  matrix products: 17.5 us -> 10.5 us
    ppermute x0 -> x29, waiting for transfers between devices: none -> 140 us  [the longest x5 63.8 us: outward(): return lax.ppermute(value, 'row', [(1, 0), (2, 3)])]
    all_gather x2 -> x0, waiting for transfers between devices: 134 us -> none  [the longest x1 77.4 us: body(): lax.all_gather(up_weight[0], 'row', axis=0, tiled=True)]
    reduce_scatter x2 -> x0, waiting for transfers between devices: 111 us -> none  [the longest x1 79.3 us: body(): lax.psum_scatter(jnp.einsum('tl,tf->lf', picked, cotangent, preferred_ele...]
    ppermute x0 -> x29, starting transfers between devices: none -> 49.4 us  [the longest x6 27 us: inward(): return lax.ppermute(value, 'row', [(0, 1), (3, 2)])]
    psum x1 -> x0, waiting for transfers between devices: 24.5 us -> none  [body(): lax.psum(latent_part.astype(jnp.bfloat16), 'col').astype(jnp.float32)]
    ppermute x1, waiting for transfers between devices: 11.6 us -> 0.01 us  [shifted(): lax.ppermute(value, axis, [(source, source + steps) for source in range(l...]
    dot_general x5 -> x14, matrix products: 17.5 us -> 10.5 us  [the longest x8 5.4 us: tokens_dot(): lax.dot_general(left, right, (((0,), (0,)), ((), ())), preferred_element_...]
  transfers between devices with their start and end apart: 6 -> 30, of which waited for: 6 -> 12; matrix products, arithmetic and copies ran while one was open for 3% -> 6% of each run, Pallas kernels for 0% -> 0%
where the time goes in v1:
time: 213 us; the launch traced here: 212 us
  waiting for transfers between devices  140 us (66%)
  starting transfers between devices  51.5 us (24%)
  matrix products  10.5 us (5%)
  other arithmetic  4.89 us (2%)
  local copies, waits for them, and re-layouts  2.92 us (1%)
    ppermute x5, waiting for transfers between devices, outward(): return lax.ppermute(value, 'row', [(1, 0), (2, 3)])  63.8 us
    ppermute x6, waiting for transfers between devices, inward(): return lax.ppermute(value, 'row', [(0, 1), (3, 2)])  54.8 us
    ppermute x6, starting transfers between devices, inward(): return lax.ppermute(value, 'row', [(0, 1), (3, 2)])  27 us
    ppermute x1, waiting for transfers between devices, folded_body(): lax.ppermute(input_grad[rows:], ('section', 'row'), [(4 * s + source, 4 *...  17.9 us
    ppermute x14, starting transfers between devices, across(): return lax.ppermute(value, 'row', [(1, 2), (2, 1)])  10.8 us
    ppermute x5, starting transfers between devices, outward(): return lax.ppermute(value, 'row', [(1, 0), (2, 3)])  6.7 us
    dot_general x8, matrix products, tokens_dot(): lax.dot_general(left, right, (((0,), (0,)), ((), ())), preferred_element_...  5.4 us
  transfers between devices with their start and end apart: 30, of which 12 were waited for; matrix products, arithmetic and copies ran while one was open for 6% of the time, Pallas kernels for 0%

profile of v1, /device:TPU:4, one launch (start us, length us, event | category | flops | bytes accessed | tf_op | source)
XLA Modules:
  0.0 211.6 jit_solution(3015508310161527184)
XLA Ops:
  0.6 1.6 fusion.39
  2.5 3.5 %collective-permute-start.8 = (bf16[320,1024]{1,0:T(8,128)(2,1)S(1)}, bf16[320,1024]{1,0:T(8,128)(2,1)S(1)}, u32[]{:S(2)}, u32[]{:S(2)}) collective-permute-start(bf16[320,1024]{1,0:T(8,128)(2,1)S(1)} %pad_maximum_fusion.8), channel_id=1, source_target_pairs={{0,2},{6,4},{1,3},{7,5},{8,10},{14,12},{9,11},{15,13},{16,18},{22,... | collective-permute-start | bytes 1966088 | tf_op jit(solution)/shard_map/ppermute | solution.py:49
  6.1 1.5 collective-permute-start.11
  7.6 1.3 collective-permute-start.14
  8.9 0.7 collective-permute-start.9
  9.6 0.7 collective-permute-start.12
  10.4 10.7 %collective-permute-done.8 = bf16[320,1024]{1,0:T(8,128)(2,1)S(1)} collective-permute-done((bf16[320,1024]{1,0:T(8,128)(2,1)S(1)}, bf16[320,1024]{1,0:T(8,128)(2,1)S(1)}, u32[]{:S(2)}, u32[]{:S(2)}) %collective-permute-start.8) | collective-permute-done | bytes 655392 | tf_op jit(solution)/shard_map/ppermute | solution.py:49
  21.1 4.4 %collective-permute-start.5 = (bf16[320,1024]{1,0:T(8,128)(2,1)S(1)}, bf16[320,1024]{1,0:T(8,128)(2,1)S(1)}, u32[]{:S(2)}, u32[]{:S(2)}) collective-permute-start(bf16[320,1024]{1,0:T(8,128)(2,1)S(1)} %pad_maximum_fusion.7), channel_id=1, source_target_pairs={{0,2},{6,4},{1,3},{7,5},{8,10},{14,12},{9,11},{15,13},{16,18},{22,... | collective-permute-start | bytes 1966088 | tf_op jit(solution)/shard_map/ppermute | solution.py:49
  25.6 0.7 collective-permute-start.15
  26.3 0.7 collective-permute-start.10
  27.0 8.2 %collective-permute-done.11 = bf16[320,1024]{1,0:T(8,128)(2,1)S(1)} collective-permute-done((bf16[320,1024]{1,0:T(8,128)(2,1)S(1)}, bf16[320,1024]{1,0:T(8,128)(2,1)S(1)}, u32[]{:S(2)}, u32[]{:S(2)}) %collective-permute-start.11) | collective-permute-done | bytes 655392 | tf_op jit(solution)/shard_map/ppermute | solution.py:49
  35.1 4.4 %collective-permute-start.1 = (bf16[128,2560]{1,0:T(8,128)(2,1)S(1)}, bf16[128,2560]{1,0:T(8,128)(2,1)S(1)}, u32[]{:S(2)}, u32[]{:S(2)}) collective-permute-start(bf16[128,2560]{1,0:T(8,128)(2,1)S(1)} %bitcast.19), channel_id=1, source_target_pairs={{0,2},{6,4},{1,3},{7,5},{8,10},{14,12},{9,11},{15,13},{16,18},{22,... | collective-permute-start | bytes 1966088 | tf_op jit(solution)/shard_map/ppermute | solution.py:49
  39.6 9.6 %collective-permute-done.14 = bf16[320,1024]{1,0:T(8,128)(2,1)S(1)} collective-permute-done((bf16[320,1024]{1,0:T(8,128)(2,1)S(1)}, bf16[320,1024]{1,0:T(8,128)(2,1)S(1)}, u32[]{:S(2)}, u32[]{:S(2)}) %collective-permute-start.14) | collective-permute-done | bytes 655392 | tf_op jit(solution)/shard_map/ppermute | solution.py:49
  49.2 0.7 collective-permute-start.13
  49.9 13.3 %collective-permute-done.5 = bf16[320,1024]{1,0:T(8,128)(2,1)S(1)} collective-permute-done((bf16[320,1024]{1,0:T(8,128)(2,1)S(1)}, bf16[320,1024]{1,0:T(8,128)(2,1)S(1)}, u32[]{:S(2)}, u32[]{:S(2)}) %collective-permute-start.5) | collective-permute-done | bytes 655392 | tf_op jit(solution)/shard_map/ppermute | solution.py:49
  63.2 0.7 collective-permute-start.16
  64.0 0.8 collective-permute-start.6
  64.9 0.7 collective-permute-start.7
  65.6 0.6 fusion.12
  66.3 11.8 %collective-permute-start = (bf16[192,2560]{1,0:T(8,128)(2,1)S(1)}, bf16[192,2560]{1,0:T(8,128)(2,1)S(1)}, u32[]{:S(2)}, u32[]{:S(2)}) collective-permute-start(bf16[192,2560]{1,0:T(8,128)(2,1)S(1)} %bitcast.13), channel_id=1, source_target_pairs={{0,2},{6,4},{1,3},{7,5},{8,10},{14,12},{9,11},{15,13},{16,18},{22,... | collective-permute-start | bytes 2949128 | tf_op jit(solution)/shard_map/ppermute | solution.py:49
  78.1 0.6 fusion.16
  78.8 0.8 collective-permute-start.2
  79.7 0.7 collective-permute-start.3
  80.4 0.6 fusion.20
  81.1 0.6 fusion.6
  82.0 1.6 collective-permute-start.17
  83.6 0.5 collective-permute-start.18
  84.1 13.1 %collective-permute-done = bf16[192,2560]{1,0:T(8,128)(2,1)S(1)} collective-permute-done((bf16[192,2560]{1,0:T(8,128)(2,1)S(1)}, bf16[192,2560]{1,0:T(8,128)(2,1)S(1)}, u32[]{:S(2)}, u32[]{:S(2)}) %collective-permute-start) | collective-permute-done | bytes 983072 | tf_op jit(solution)/shard_map/ppermute | solution.py:49
  97.2 1.2 convolution_convert_fusion.7
  98.4 1.6 collective-permute-start.4
  100.0 0.8 convert_add_fusion.1
  100.8 1.3 collective-permute-start.19
  102.1 1.0 convert_element_type.76
  103.1 3.5 %collective-permute-done.4 = bf16[384,512]{1,0:T(8,128)(2,1)S(1)} collective-permute-done((bf16[384,512]{1,0:T(8,128)(2,1)S(1)}, bf16[384,512]{1,0:T(8,128)(2,1)S(1)}, u32[]{:S(2)}, u32[]{:S(2)}) %collective-permute-start.4) | collective-permute-done | bytes 393248 | tf_op jit(solution)/shard_map/ppermute | solution.py:61
  106.8 0.3 multiply_reduce_fusion
  107.1 0.2 fusion.8
  107.4 0.8 collective-permute-start.25
  108.3 0.3 copy-done.11
  108.6 0.5 convolution_convert_fusion.1
  109.1 0.8 collective-permute-start.23
  110.0 0.5 convolution_convert_fusion.2
  110.5 0.7 collective-permute-start.22
  111.3 1.4 convolution_convert_fusion
  112.8 2.1 collective-permute-start.20
  115.0 0.6 convolution_convert_fusion.6
  115.6 1.4 collective-permute-start.26
  117.1 0.6 convolution_convert_fusion.5
  117.7 1.4 collective-permute-start.27
  119.2 0.6 convolution_convert_fusion.4
  119.8 0.6 convolution_convert_fusion.3
  120.5 37.9 %collective-permute-done.26 = bf16[128,1024]{1,0:T(8,128)(2,1)S(1)} collective-permute-done((bf16[128,1024]{1,0:T(8,128)(2,1)S(1)}, bf16[128,1024]{1,0:T(8,128)(2,1)S(1)}, u32[]{:S(2)}, u32[]{:S(2)}) %collective-permute-start.26) | collective-permute-done | bytes 262176 | tf_op jit(solution)/shard_map/ppermute | solution.py:57
  158.3 1.3 collective-permute-start.28
  159.6 4.3 %collective-permute-done.27 = bf16[128,1024]{1,0:T(8,128)(2,1)S(1)} collective-permute-done((bf16[128,1024]{1,0:T(8,128)(2,1)S(1)}, bf16[128,1024]{1,0:T(8,128)(2,1)S(1)}, u32[]{:S(2)}, u32[]{:S(2)}) %collective-permute-start.27) | collective-permute-done | bytes 262176 | tf_op jit(solution)/shard_map/ppermute | solution.py:57
  163.9 1.3 collective-permute-start.29
  165.3 4.3 %collective-permute-done.28 = bf16[128,1024]{1,0:T(8,128)(2,1)S(1)} collective-permute-done((bf16[128,1024]{1,0:T(8,128)(2,1)S(1)}, bf16[128,1024]{1,0:T(8,128)(2,1)S(1)}, u32[]{:S(2)}, u32[]{:S(2)}) %collective-permute-start.28) | collective-permute-done | bytes 262176 | tf_op jit(solution)/shard_map/ppermute | solution.py:57
  169.6 1.3 collective-permute-start.21
  170.9 4.3 %collective-permute-done.29 = bf16[128,1024]{1,0:T(8,128)(2,1)S(1)} collective-permute-done((bf16[128,1024]{1,0:T(8,128)(2,1)S(1)}, bf16[128,1024]{1,0:T(8,128)(2,1)S(1)}, u32[]{:S(2)}, u32[]{:S(2)}) %collective-permute-start.29) | collective-permute-done | bytes 262176 | tf_op jit(solution)/shard_map/ppermute | solution.py:57
  175.2 1.0 maximum_bitcast_fusion
  176.2 0.5 fusion.1
  176.8 1.3 collective-permute-start.24
  178.1 17.9 %collective-permute-done.21 = bf16[192,2560]{1,0:T(8,128)(2,1)S(1)} collective-permute-done((bf16[192,2560]{1,0:T(8,128)(2,1)S(1)}, bf16[192,2560]{1,0:T(8,128)(2,1)S(1)}, u32[]{:S(2)}, u32[]{:S(2)}) %collective-permute-start.21) | collective-permute-done | bytes 983072 | tf_op jit(solution)/shard_map/ppermute | solution.py:141
  196.0 1.0 select_bitcast_fusion
  197.0 13.1 %collective-permute-done.24 = bf16[128,2560]{1,0:T(8,128)(2,1)S(1)} collective-permute-done((bf16[128,2560]{1,0:T(8,128)(2,1)S(1)}, bf16[128,2560]{1,0:T(8,128)(2,1)S(1)}, u32[]{:S(2)}, u32[]{:S(2)}) %collective-permute-start.24) | collective-permute-done | bytes 655392 | tf_op jit(solution)/shard_map/ppermute | solution.py:57
  210.1 1.4 fusion.3
  (119 shorter events, 1.6 us)
Async XLA Ops:
  0.6 1.7 copy-start
  2.5 18.6 %collective-permute-start.8 = (bf16[320,1024]{1,0:T(8,128)(2,1)S(1)}, bf16[320,1024]{1,0:T(8,128)(2,1)S(1)}, u32[]{:S(2)}, u32[]{:S(2)}) collective-permute-start(bf16[320,1024]{1,0:T(8,128)(2,1)S(1)} %pad_maximum_fusion.8), channel_id=1, source_target_pairs={{0,2},{6,4},{1,3},{7,5},{8,10},{14,12},{9,11},{15,13},{16,18},{22,... | collective-permute-start | bytes 1966088 | tf_op jit(solution)/shard_map/ppermute | solution.py:49
  6.1 29.1 %copy-start.12 = (bf16[1,128,2560]{2,1,0:T(8,128)(2,1)S(1)}, bf16[1,128,2560]{2,1,0:T(8,128)(2,1)}, u32[]{:S(2)}) copy-start(bf16[1,128,2560]{2,1,0:T(8,128)(2,1)} %param.5) | copy-start | bytes 1966084
  6.1 29.1 %collective-permute-start.11 = (bf16[320,1024]{1,0:T(8,128)(2,1)S(1)}, bf16[320,1024]{1,0:T(8,128)(2,1)S(1)}, u32[]{:S(2)}, u32[]{:S(2)}) collective-permute-start(bf16[320,1024]{1,0:T(8,128)(2,1)S(1)} %pad_maximum_fusion.9), channel_id=1, source_target_pairs={{0,2},{6,4},{1,3},{7,5},{8,10},{14,12},{9,11},{15,13},{16,18},{22,... | collective-permute-start | bytes 1966088 | tf_op jit(solution)/shard_map/ppermute | solution.py:49
  7.6 41.6 %collective-permute-start.14 = (bf16[320,1024]{1,0:T(8,128)(2,1)S(1)}, bf16[320,1024]{1,0:T(8,128)(2,1)S(1)}, u32[]{:S(2)}, u32[]{:S(2)}) collective-permute-start(bf16[320,1024]{1,0:T(8,128)(2,1)S(1)} %pad_maximum_fusion.10), channel_id=1, source_target_pairs={{0,2},{6,4},{1,3},{7,5},{8,10},{14,12},{9,11},{15,13},{16,18},{22,... | collective-permute-start | bytes 1966088 | tf_op jit(solution)/shard_map/ppermute | solution.py:49
  8.9 16.6 %collective-permute-start.9 = (bf16[192,1024]{1,0:T(8,128)(2,1)S(1)}, bf16[192,1024]{1,0:T(8,128)(2,1)S(1)}, u32[]{:S(2)}, u32[]{:S(2)}) collective-permute-start(bf16[192,1024]{1,0:T(8,128)(2,1)S(1)} %get-tuple-element.8), channel_id=1, source_target_pairs={{2,4},{4,2},{3,5},{5,3},{10,12},{12,10},{11,13},{13,11},{18,20},{2... | collective-permute-start | bytes 1179656 | tf_op jit(solution)/shard_map/ppermute | solution.py:53
  9.6 16.6 %collective-permute-start.12 = (bf16[192,1024]{1,0:T(8,128)(2,1)S(1)}, bf16[192,1024]{1,0:T(8,128)(2,1)S(1)}, u32[]{:S(2)}, u32[]{:S(2)}) collective-permute-start(bf16[192,1024]{1,0:T(8,128)(2,1)S(1)} %get-tuple-element.7), channel_id=1, source_target_pairs={{2,4},{4,2},{3,5},{5,3},{10,12},{12,10},{11,13},{13,11},{18,20},{2... | collective-permute-start | bytes 1179656 | tf_op jit(solution)/shard_map/ppermute | solution.py:53
  21.1 42.1 %collective-permute-start.5 = (bf16[320,1024]{1,0:T(8,128)(2,1)S(1)}, bf16[320,1024]{1,0:T(8,128)(2,1)S(1)}, u32[]{:S(2)}, u32[]{:S(2)}) collective-permute-start(bf16[320,1024]{1,0:T(8,128)(2,1)S(1)} %pad_maximum_fusion.7), channel_id=1, source_target_pairs={{0,2},{6,4},{1,3},{7,5},{8,10},{14,12},{9,11},{15,13},{16,18},{22,... | collective-permute-start | bytes 1966088 | tf_op jit(solution)/shard_map/ppermute | solution.py:49
  25.6 40.0 %copy-start.22 = (bf16[192,1024]{1,0:T(8,128)(2,1)}, bf16[192,1024]{1,0:T(8,128)(2,1)S(1)}, u32[]{:S(2)}) copy-start(bf16[192,1024]{1,0:T(8,128)(2,1)S(1)} %collective-permute-done.9) | copy-start | bytes 1179652
  25.6 38.4 %collective-permute-start.15 = (bf16[192,1024]{1,0:T(8,128)(2,1)S(1)}, bf16[192,1024]{1,0:T(8,128)(2,1)S(1)}, u32[]{:S(2)}, u32[]{:S(2)}) collective-permute-start(bf16[192,1024]{1,0:T(8,128)(2,1)S(1)} %get-tuple-element.6), channel_id=1, source_target_pairs={{2,4},{4,2},{3,5},{5,3},{10,12},{12,10},{11,13},{13,11},{18,20},{2... | collective-permute-start | bytes 1179656 | tf_op jit(solution)/shard_map/ppermute | solution.py:53
  26.3 51.9 %copy-start.20 = (bf16[192,1024]{1,0:T(8,128)(2,1)}, bf16[192,1024]{1,0:T(8,128)(2,1)S(1)}, u32[]{:S(2)}) copy-start(bf16[192,1024]{1,0:T(8,128)(2,1)S(1)} %collective-permute-done.12) | copy-start | bytes 1179652
  26.3 38.6 %collective-permute-start.10 = (bf16[192,1024]{1,0:T(8,128)(2,1)S(1)}, bf16[192,1024]{1,0:T(8,128)(2,1)S(1)}, u32[]{:S(2)}, u32[]{:S(2)}) collective-permute-start(bf16[192,1024]{1,0:T(8,128)(2,1)S(1)} %slice.152), channel_id=1, source_target_pairs={{2,4},{4,2},{3,5},{5,3},{10,12},{12,10},{11,13},{13,11},{18,20},{2... | collective-permute-start | bytes 1179656 | tf_op jit(solution)/shard_map/ppermute | solution.py:53
  35.1 28.8 %copy-start.1 = (bf16[320,1024]{1,0:T(8,128)(2,1)}, bf16[320,1024]{1,0:T(8,128)(2,1)S(1)}, u32[]{:S(2)}) copy-start(bf16[320,1024]{1,0:T(8,128)(2,1)S(1)} %collective-permute-done.11) | copy-start | bytes 1966084
  35.1 43.7 %collective-permute-start.1 = (bf16[128,2560]{1,0:T(8,128)(2,1)S(1)}, bf16[128,2560]{1,0:T(8,128)(2,1)S(1)}, u32[]{:S(2)}, u32[]{:S(2)}) collective-permute-start(bf16[128,2560]{1,0:T(8,128)(2,1)S(1)} %bitcast.19), channel_id=1, source_target_pairs={{0,2},{6,4},{1,3},{7,5},{8,10},{14,12},{9,11},{15,13},{16,18},{22,... | collective-permute-start | bytes 1966088 | tf_op jit(solution)/shard_map/ppermute | solution.py:49
  49.2 17.0 %copy-start.2 = (bf16[320,1024]{1,0:T(8,128)(2,1)}, bf16[320,1024]{1,0:T(8,128)(2,1)S(1)}, u32[]{:S(2)}) copy-start(bf16[320,1024]{1,0:T(8,128)(2,1)S(1)} %collective-permute-done.14) | copy-start | bytes 1966084
  49.2 17.1 %collective-permute-start.13 = (bf16[192,1024]{1,0:T(8,128)(2,1)S(1)}, bf16[192,1024]{1,0:T(8,128)(2,1)S(1)}, u32[]{:S(2)}, u32[]{:S(2)}) collective-permute-start(bf16[192,1024]{1,0:T(8,128)(2,1)S(1)} %slice.156), channel_id=1, source_target_pairs={{2,4},{4,2},{3,5},{5,3},{10,12},{12,10},{11,13},{13,11},{18,20},{2... | collective-permute-start | bytes 1179656 | tf_op jit(solution)/shard_map/ppermute | solution.py:53
  49.9 30.5 %copy-start.4 = (bf16[192,1024]{1,0:T(8,128)(2,1)}, bf16[192,1024]{1,0:T(8,128)(2,1)S(1)}, u32[]{:S(2)}) copy-start(bf16[192,1024]{1,0:T(8,128)(2,1)S(1)} %slice.160) | copy-start | bytes 1179652
  63.2 3.0 %copy-start.3 = (bf16[320,1024]{1,0:T(8,128)(2,1)}, bf16[320,1024]{1,0:T(8,128)(2,1)S(1)}, u32[]{:S(2)}) copy-start(bf16[320,1024]{1,0:T(8,128)(2,1)S(1)} %collective-permute-done.5) | copy-start | bytes 1966084
  63.2 16.4 %collective-permute-start.16 = (bf16[192,1024]{1,0:T(8,128)(2,1)S(1)}, bf16[192,1024]{1,0:T(8,128)(2,1)S(1)}, u32[]{:S(2)}, u32[]{:S(2)}) collective-permute-start(bf16[192,1024]{1,0:T(8,128)(2,1)S(1)} %slice.160), channel_id=1, source_target_pairs={{2,4},{4,2},{3,5},{5,3},{10,12},{12,10},{11,13},{13,11},{18,20},{2... | collective-permute-start | bytes 1179656 | tf_op jit(solution)/shard_map/ppermute | solution.py:53
  64.0 17.1 %copy-start.6 = (bf16[192,1024]{1,0:T(8,128)(2,1)}, bf16[192,1024]{1,0:T(8,128)(2,1)S(1)}, u32[]{:S(2)}) copy-start(bf16[192,1024]{1,0:T(8,128)(2,1)S(1)} %slice.148) | copy-start | bytes 1179652
  64.0 2.3 %copy-start.8 = (bf16[1,192,2560]{2,1,0:T(8,128)(2,1)S(1)}, bf16[1,192,2560]{2,1,0:T(8,128)(2,1)}, u32[]{:S(2)}) copy-start(bf16[1,192,2560]{2,1,0:T(8,128)(2,1)} %param.4) | copy-start | bytes 2949124
  64.0 14.1 %slice-start = ((bf16[320,1024]{1,0:T(8,128)(2,1)}), bf16[128,1024]{1,0:T(8,128)(2,1)S(1)}, s32[]{:S(2)}) async-start(bf16[320,1024]{1,0:T(8,128)(2,1)} %copy-done.1), calls=%async_computation | async-start | bytes 524288 | tf_op jit(solution)/shard_map/slice | solution.py:101
  64.0 16.4 %copy-start.24 = (bf16[192,1024]{1,0:T(8,128)(2,1)}, bf16[192,1024]{1,0:T(8,128)(2,1)S(1)}, u32[]{:S(2)}) copy-start(bf16[192,1024]{1,0:T(8,128)(2,1)S(1)} %collective-permute-done.15) | copy-start | bytes 1179652
  64.0 17.0 %collective-permute-start.6 = (bf16[192,1024]{1,0:T(8,128)(2,1)S(1)}, bf16[192,1024]{1,0:T(8,128)(2,1)S(1)}, u32[]{:S(2)}, u32[]{:S(2)}) collective-permute-start(bf16[192,1024]{1,0:T(8,128)(2,1)S(1)} %get-tuple-element.5), channel_id=1, source_target_pairs={{2,4},{4,2},{3,5},{5,3},{10,12},{12,10},{11,13},{13,11},{18,20},{2... | collective-permute-start | bytes 1179656 | tf_op jit(solution)/shard_map/ppermute | solution.py:53
  64.9 1.4 copy-start.26
  64.9 16.2 %collective-permute-start.7 = (bf16[192,1024]{1,0:T(8,128)(2,1)S(1)}, bf16[192,1024]{1,0:T(8,128)(2,1)S(1)}, u32[]{:S(2)}, u32[]{:S(2)}) collective-permute-start(bf16[192,1024]{1,0:T(8,128)(2,1)S(1)} %slice.148), channel_id=1, source_target_pairs={{2,4},{4,2},{3,5},{5,3},{10,12},{12,10},{11,13},{13,11},{18,20},{2... | collective-permute-start | bytes 1179656 | tf_op jit(solution)/shard_map/ppermute | solution.py:53
  66.2 12.5 %copy-start.28 = (bf16[192,1024]{1,0:T(8,128)(2,1)}, bf16[192,1024]{1,0:T(8,128)(2,1)S(1)}, u32[]{:S(2)}) copy-start(bf16[192,1024]{1,0:T(8,128)(2,1)S(1)} %collective-permute-done.13) | copy-start | bytes 1179652
  66.3 14.2 %slice-start.1 = ((bf16[320,1024]{1,0:T(8,128)(2,1)}), bf16[128,1024]{1,0:T(8,128)(2,1)S(1)}, s32[]{:S(2)}) async-start(bf16[320,1024]{1,0:T(8,128)(2,1)} %copy-done.2), calls=%async_computation.1 | async-start | bytes 524288 | tf_op jit(solution)/shard_map/slice | solution.py:101
  66.3 30.9 %collective-permute-start = (bf16[192,2560]{1,0:T(8,128)(2,1)S(1)}, bf16[192,2560]{1,0:T(8,128)(2,1)S(1)}, u32[]{:S(2)}, u32[]{:S(2)}) collective-permute-start(bf16[192,2560]{1,0:T(8,128)(2,1)S(1)} %bitcast.13), channel_id=1, source_target_pairs={{0,2},{6,4},{1,3},{7,5},{8,10},{14,12},{9,11},{15,13},{16,18},{22,... | collective-permute-start | bytes 2949128 | tf_op jit(solution)/shard_map/ppermute | solution.py:49
  78.8 2.3 %slice-start.2 = ((bf16[320,1024]{1,0:T(8,128)(2,1)}), bf16[128,1024]{1,0:T(8,128)(2,1)S(1)}, s32[]{:S(2)}) async-start(bf16[320,1024]{1,0:T(8,128)(2,1)} %copy-done.3), calls=%async_computation.2 | async-start | bytes 524288 | tf_op jit(solution)/shard_map/slice | solution.py:101
  78.8 18.4 %copy-start.14 = (bf16[128,2560]{1,0:T(8,128)(2,1)}, bf16[128,2560]{1,0:T(8,128)(2,1)S(1)}, u32[]{:S(2)}) copy-start(bf16[128,2560]{1,0:T(8,128)(2,1)S(1)} %collective-permute-done.1) | copy-start | bytes 1966084
  78.8 5.3 %collective-permute-start.2 = (bf16[128,2560]{1,0:T(8,128)(2,1)S(1)}, bf16[128,2560]{1,0:T(8,128)(2,1)S(1)}, u32[]{:S(2)}, u32[]{:S(2)}) collective-permute-start(bf16[128,2560]{1,0:T(8,128)(2,1)S(1)} %bitcast.20), channel_id=1, source_target_pairs={{2,4},{4,2},{3,5},{5,3},{10,12},{12,10},{11,13},{13,11},{18,20},{2... | collective-permute-start | bytes 1966088 | tf_op jit(solution)/shard_map/ppermute | solution.py:53
  79.7 1.4 copy-start.30
  79.7 17.5 %collective-permute-start.3 = (bf16[128,2560]{1,0:T(8,128)(2,1)S(1)}, bf16[128,2560]{1,0:T(8,128)(2,1)S(1)}, u32[]{:S(2)}, u32[]{:S(2)}) collective-permute-start(bf16[128,2560]{1,0:T(8,128)(2,1)S(1)} %collective-permute-done.1), channel_id=1, source_target_pairs={{2,4},{4,2},{3,5},{5,3},{10,12},{12,10},{11,13},{13,11},{18,20},{2... | collective-permute-start | bytes 1966088 | tf_op jit(solution)/shard_map/ppermute | solution.py:53
  82.0 18.0 %collective-permute-start.17 = (bf16[384,256]{1,0:T(8,128)(2,1)S(1)}, bf16[384,256]{1,0:T(8,128)(2,1)S(1)}, u32[]{:S(2)}, u32[]{:S(2)}) collective-permute-start(bf16[384,256]{1,0:T(8,128)(2,1)S(1)} %get-tuple-element.19), channel_id=1, source_target_pairs={{0,1},{1,0},{2,3},{3,2},{4,5},{5,4},{6,7},{7,6},{8,9},{9,8},{10,11... | collective-permute-start | bytes 589832 | tf_op jit(solution)/shard_map/ppermute | solution.py:61
  83.6 16.4 %collective-permute-start.18 = (bf16[384,256]{1,0:T(8,128)(2,1)S(1)}, bf16[384,256]{1,0:T(8,128)(2,1)S(1)}, u32[]{:S(2)}, u32[]{:S(2)}) collective-permute-start(bf16[384,256]{1,0:T(8,128)(2,1)S(1)} %get-tuple-element.20), channel_id=1, source_target_pairs={{0,1},{1,0},{2,3},{3,2},{4,5},{5,4},{6,7},{7,6},{8,9},{9,8},{10,11... | collective-permute-start | bytes 589832 | tf_op jit(solution)/shard_map/ppermute | solution.py:61
  84.1 14.3 %copy-start.16 = (bf16[128,2560]{1,0:T(8,128)(2,1)}, bf16[128,2560]{1,0:T(8,128)(2,1)S(1)}, u32[]{:S(2)}) copy-start(bf16[128,2560]{1,0:T(8,128)(2,1)S(1)} %collective-permute-done.2) | copy-start | bytes 1966084
  98.4 8.1 %collective-permute-start.4 = (bf16[384,512]{1,0:T(8,128)(2,1)S(1)}, bf16[384,512]{1,0:T(8,128)(2,1)S(1)}, u32[]{:S(2)}, u32[]{:S(2)}) collective-permute-start(bf16[384,512]{1,0:T(8,128)(2,1)S(1)} %convolution_convert_fusion.7), channel_id=1, source_target_pairs={{0,1},{1,0},{2,3},{3,2},{4,5},{5,4},{6,7},{7,6},{8,9},{9,8},{10,11... | collective-permute-start | bytes 1179656 | tf_op jit(solution)/shard_map/ppermute | solution.py:61
  100.8 1.3 collective-permute-start.19
  107.1 1.5 copy-start.11
  107.4 7.5 %collective-permute-start.25 = (bf16[384,256]{1,0:T(8,128)(2,1)S(1)}, bf16[384,256]{1,0:T(8,128)(2,1)S(1)}, u32[]{:S(2)}, u32[]{:S(2)}) collective-permute-start(bf16[384,256]{1,0:T(8,128)(2,1)S(1)} %get-tuple-element.16), channel_id=1, source_target_pairs={{2,4},{4,2},{3,5},{5,3},{10,12},{12,10},{11,13},{13,11},{18,20},{2... | collective-permute-start | bytes 589832 | tf_op jit(solution)/shard_map/ppermute | solution.py:53
  109.1 2.1 %copy-start.13 = (bf16[1,128,2560]{2,1,0:T(8,128)(2,1)S(1)}, bf16[1,128,2560]{2,1,0:T(8,128)(2,1)}, u32[]{:S(2)}) copy-start(bf16[1,128,2560]{2,1,0:T(8,128)(2,1)} %param.5) | copy-start | bytes 1966084
  109.1 2.1 %copy-start.15 = (bf16[128,2560]{1,0:T(8,128)(2,1)S(1)}, bf16[128,2560]{1,0:T(8,128)(2,1)}, u32[]{:S(2)}) copy-start(bf16[128,2560]{1,0:T(8,128)(2,1)} %copy-done.14) | copy-start | bytes 1966084
  109.1 2.1 %copy-start.17 = (bf16[128,2560]{1,0:T(8,128)(2,1)S(1)}, bf16[128,2560]{1,0:T(8,128)(2,1)}, u32[]{:S(2)}) copy-start(bf16[128,2560]{1,0:T(8,128)(2,1)} %copy-done.16) | copy-start | bytes 1966084
  109.1 2.1 %copy-start.19 = (bf16[128,2560]{1,0:T(8,128)(2,1)S(1)}, bf16[128,2560]{1,0:T(8,128)(2,1)}, u32[]{:S(2)}) copy-start(bf16[128,2560]{1,0:T(8,128)(2,1)} %copy-done.18) | copy-start | bytes 1966084
  109.1 67.1 %collective-permute-start.23 = (bf16[128,2560]{1,0:T(8,128)(2,1)S(1)}, bf16[128,2560]{1,0:T(8,128)(2,1)S(1)}, u32[]{:S(2)}, u32[]{:S(2)}) collective-permute-start(bf16[128,2560]{1,0:T(8,128)(2,1)S(1)} %convolution_convert_fusion.1), channel_id=1, source_target_pairs={{2,4},{4,2},{3,5},{5,3},{10,12},{12,10},{11,13},{13,11},{18,20},{2... | collective-permute-start | bytes 1966088 | tf_op jit(solution)/shard_map/ppermute | solution.py:53
  110.5 86.5 %collective-permute-start.22 = (bf16[128,2560]{1,0:T(8,128)(2,1)S(1)}, bf16[128,2560]{1,0:T(8,128)(2,1)S(1)}, u32[]{:S(2)}, u32[]{:S(2)}) collective-permute-start(bf16[128,2560]{1,0:T(8,128)(2,1)S(1)} %convolution_convert_fusion.2), channel_id=1, source_target_pairs={{2,4},{4,2},{3,5},{5,3},{10,12},{12,10},{11,13},{13,11},{18,20},{2... | collective-permute-start | bytes 1966088 | tf_op jit(solution)/shard_map/ppermute | solution.py:53
  112.7 2.2 %copy-start.7 = (bf16[192,1024]{1,0:T(8,128)(2,1)S(1)}, bf16[192,1024]{1,0:T(8,128)(2,1)}, u32[]{:S(2)}) copy-start(bf16[192,1024]{1,0:T(8,128)(2,1)} %copy-done.6) | copy-start | bytes 1179652
  112.7 2.2 %copy-start.33 = (bf16[192,1024]{1,0:T(8,128)(2,1)S(1)}, bf16[192,1024]{1,0:T(8,128)(2,1)}, u32[]{:S(2)}) copy-start(bf16[192,1024]{1,0:T(8,128)(2,1)} %copy-done.32) | copy-start | bytes 1179652
  112.7 2.2 %copy-start.35 = (bf16[192,1024]{1,0:T(8,128)(2,1)S(1)}, bf16[192,1024]{1,0:T(8,128)(2,1)}, u32[]{:S(2)}) copy-start(bf16[192,1024]{1,0:T(8,128)(2,1)} %copy-done.34) | copy-start | bytes 1179652
  112.8 65.2 %collective-permute-start.20 = (bf16[192,2560]{1,0:T(8,128)(2,1)S(1)}, bf16[192,2560]{1,0:T(8,128)(2,1)S(1)}, u32[]{:S(2)}, u32[]{:S(2)}) collective-permute-start(bf16[192,2560]{1,0:T(8,128)(2,1)S(1)} %get-tuple-element.4), channel_id=1, source_target_pairs={{8,0},{16,8},{24,16},{9,1},{17,9},{25,17},{10,2},{18,10},{26,18},{... | collective-permute-start | bytes 2949128 | tf_op jit(solution)/shard_map/ppermute | solution.py:14
  115.0 2.1 copy-start.23
  115.0 2.1 copy-start.27
  115.6 3.6 %copy-start.21 = (bf16[192,1024]{1,0:T(8,128)(2,1)S(1)}, bf16[192,1024]{1,0:T(8,128)(2,1)}, u32[]{:S(2)}) copy-start(bf16[192,1024]{1,0:T(8,128)(2,1)} %copy-done.20) | copy-start | bytes 1179652
  115.6 3.6 %copy-start.29 = (bf16[192,1024]{1,0:T(8,128)(2,1)S(1)}, bf16[192,1024]{1,0:T(8,128)(2,1)}, u32[]{:S(2)}) copy-start(bf16[192,1024]{1,0:T(8,128)(2,1)} %copy-done.28) | copy-start | bytes 1179652
  115.6 42.7 %collective-permute-start.26 = (bf16[128,1024]{1,0:T(8,128)(2,1)S(1)}, bf16[128,1024]{1,0:T(8,128)(2,1)S(1)}, u32[]{:S(2)}, u32[]{:S(2)}) collective-permute-start(bf16[128,1024]{1,0:T(8,128)(2,1)S(1)} %slice.173), channel_id=1, source_target_pairs={{2,0},{4,6},{3,1},{5,7},{10,8},{12,14},{11,9},{13,15},{18,16},{20,... | collective-permute-start | bytes 786440 | tf_op jit(solution)/shard_map/ppermute | solution.py:57
  117.7 2.1 copy-start.5
  117.7 2.1 copy-start.25
  117.7 2.1 copy-start.31
  117.7 46.2 %collective-permute-start.27 = (bf16[128,1024]{1,0:T(8,128)(2,1)S(1)}, bf16[128,1024]{1,0:T(8,128)(2,1)S(1)}, u32[]{:S(2)}, u32[]{:S(2)}) collective-permute-start(bf16[128,1024]{1,0:T(8,128)(2,1)S(1)} %slice.175), channel_id=1, source_target_pairs={{2,0},{4,6},{3,1},{5,7},{10,8},{12,14},{11,9},{13,15},{18,16},{20,... | collective-permute-start | bytes 786440 | tf_op jit(solution)/shard_map/ppermute | solution.py:57
  158.3 11.2 %collective-permute-start.28 = (bf16[128,1024]{1,0:T(8,128)(2,1)S(1)}, bf16[128,1024]{1,0:T(8,128)(2,1)S(1)}, u32[]{:S(2)}, u32[]{:S(2)}) collective-permute-start(bf16[128,1024]{1,0:T(8,128)(2,1)S(1)} %slice.177), channel_id=1, source_target_pairs={{2,0},{4,6},{3,1},{5,7},{10,8},{12,14},{11,9},{13,15},{18,16},{20,... | collective-permute-start | bytes 786440 | tf_op jit(solution)/shard_map/ppermute | solution.py:57
  163.9 11.2 %collective-permute-start.29 = (bf16[128,1024]{1,0:T(8,128)(2,1)S(1)}, bf16[128,1024]{1,0:T(8,128)(2,1)S(1)}, u32[]{:S(2)}, u32[]{:S(2)}) collective-permute-start(bf16[128,1024]{1,0:T(8,128)(2,1)S(1)} %slice.179), channel_id=1, source_target_pairs={{2,0},{4,6},{3,1},{5,7},{10,8},{12,14},{11,9},{13,15},{18,16},{20,... | collective-permute-start | bytes 786440 | tf_op jit(solution)/shard_map/ppermute | solution.py:57
  169.6 26.4 %collective-permute-start.21 = (bf16[192,2560]{1,0:T(8,128)(2,1)S(1)}, bf16[192,2560]{1,0:T(8,128)(2,1)S(1)}, u32[]{:S(2)}, u32[]{:S(2)}) collective-permute-start(bf16[192,2560]{1,0:T(8,128)(2,1)S(1)} %get-tuple-element.3), channel_id=1, source_target_pairs={{10,0},{12,6},{18,8},{20,14},{26,16},{28,22},{11,1},{13,7},{19,9},... | collective-permute-start | bytes 2949128 | tf_op jit(solution)/shard_map/ppermute | solution.py:141
  176.8 33.4 %collective-permute-start.24 = (bf16[128,2560]{1,0:T(8,128)(2,1)S(1)}, bf16[128,2560]{1,0:T(8,128)(2,1)S(1)}, u32[]{:S(2)}, u32[]{:S(2)}) collective-permute-start(bf16[128,2560]{1,0:T(8,128)(2,1)S(1)} %fusion.1), channel_id=1, source_target_pairs={{2,0},{4,6},{3,1},{5,7},{10,8},{12,14},{11,9},{13,15},{18,16},{20,... | collective-permute-start | bytes 1966088 | tf_op jit(solution)/shard_map/ppermute | solution.py:57
  (5 other events, 5.3 us)
